TPU v7x, 256 devices: a whole 4x4x8 slice. The times are simulated.
256 devices in a mesh: example: 64 (over x, z, core), feature: 4 (over y).
Axes of the slice: x: 4, y: 4, z: 8, core: 2. Of those that a mesh axis runs over, the one named last changes fastest.
Arguments:
- embeddings: bfloat16 [36864, 16384], P('example', 'feature'), may hold values from -16 to 16
- subspace: bfloat16 [16384, 128], P('feature'), may hold values from -0.046875 to 0.046875
- noise_levels: int32 [16384, 128], P('feature'), may hold values from -16 to 16
- targets: int32 [2048], replicated, may hold values from 0 to 16383
Outputs:
- embedding_grad: bfloat16 [36864, 16384], P('example', 'feature')
All inputs are finite; a program needn't handle non-finite values.
Results may differ from a plain program's by a relative error of at most 0.0085.
Values may be sent and summed in bfloat16 or wider, within the bound.
A program may use at most 64 MiB of HBM per device.

v0:
```python
import jax
import jax.numpy as jnp
from jax import lax
from jax.sharding import PartitionSpec as P

NOISE_STEP = 1.0 / 4096.0
HIGH = lax.Precision.HIGHEST


def transposed(former, latter, precision=None):
    return lax.dot_general(
        former,
        latter,
        (((0,), (0,)), ((), ())),
        precision=precision,
        preferred_element_type=jnp.float32,
    )


def by_columns(former, latter):
    return lax.dot_general(
        former, latter, (((1,), (1,)), ((), ())), preferred_element_type=jnp.float32
    )


def count_rows(targets, first, length):
    local = targets - first
    inside = (local >= 0) & (local < length)
    slots = jnp.where(inside, local, length)
    ones = jnp.ones(targets.shape, jnp.float32)
    return jax.ops.segment_sum(ones, slots, num_segments=length + 1)[:length]


def upper_factor(gram_matrix):
    return jnp.linalg.cholesky(gram_matrix).T


def factorize(gram_matrix):
    lower_factor = jnp.linalg.cholesky(gram_matrix)
    identity = jnp.eye(gram_matrix.shape[0], dtype=jnp.float32)
    inverse_factor = jax.scipy.linalg.solve_triangular(lower_factor, identity, lower=True)
    gram_inverse = jnp.dot(inverse_factor.T, inverse_factor, precision=HIGH)
    return (inverse_factor, gram_inverse)


def on_device(embeddings, subspace, noise_levels, targets):
    row_count, local_width = embeddings.shape
    examples = lax.axis_size("example")
    total_rows = row_count * examples
    projected = lax.psum(
        jnp.dot(embeddings, subspace, preferred_element_type=jnp.float32), "feature"
    )
    projected_low = projected.astype(jnp.bfloat16)
    feature_first = lax.axis_index("feature") * local_width
    share = local_width // examples
    summed = lax.psum_scatter(
        transposed(embeddings, projected_low), "example", scatter_dimension=0, tiled=True
    )
    offset = lax.axis_index("example") * share
    noise_part = lax.dynamic_slice_in_dim(noise_levels, offset, share, 0)
    image = summed / total_rows + NOISE_STEP * noise_part.astype(jnp.float32)
    row_counts = count_rows(targets, feature_first + offset, share)
    gram_matrix = lax.psum(transposed(image, image, HIGH), ("example", "feature"))
    inverse_factor, gram_inverse = factorize(gram_matrix)
    orthonormal = jnp.dot(image, inverse_factor.T, precision=HIGH)
    alignment = lax.psum(
        transposed(orthonormal * row_counts[:, None], orthonormal, HIGH), ("example", "feature")
    )
    factor_grad = 2.0 * jnp.dot(alignment, inverse_factor, precision=HIGH)
    unused, pull_back = jax.vjp(upper_factor, gram_matrix)
    gram_grad = pull_back(factor_grad)[0]
    image_grad = jnp.dot(image, gram_grad + gram_grad.T, precision=HIGH) - 2.0 * row_counts[
        :, None
    ] * jnp.dot(image, gram_inverse, precision=HIGH)
    grad_low = image_grad.astype(jnp.bfloat16)
    grad_low = lax.all_gather(grad_low, "example", axis=0, tiled=True)
    back_sum = lax.psum(
        jnp.dot(embeddings, grad_low, preferred_element_type=jnp.float32), "feature"
    )
    back_rows = back_sum.astype(jnp.bfloat16)
    result = by_columns(projected_low, grad_low) + by_columns(back_rows, subspace)
    return result.astype(jnp.bfloat16)


def solution(mesh):
    in_specs = (P("example", "feature"), P("feature", None), P("feature", None), P())
    out_specs = P("example", "feature")
    return jax.shard_map(
        on_device, mesh=mesh, in_specs=in_specs, out_specs=out_specs, check_vma=False
    )
```

profile of v0, /device:TPU:2, one launch (start us, length us, event | category | flops | bytes accessed | tf_op | source)
XLA Modules:
  0.0 797.7 jit_solution(3288870860719686440)
XLA Ops:
  6.5 4.2 fusion.45
  10.7 20.2 %all-reduce.8 = bf16[576,128]{1,0:T(8,128)(2,1)S(1)} all-reduce(f32[576,128]{1,0:T(8,128)S(1)} %fusion.45), channel_id=1, replica_groups=mesh['example'=64,'feature'=4] {'feature'}, use_global_device_ids=true, to_apply=%region_0.0 | all-reduce | flops 73728 | bytes 442368 | tf_op jit(solution)/shard_map/psum | solution.py:50
  30.9 4.7 convolution_bitcast_fusion
  35.6 2.9 copy.14
  38.8 14.7 %scatter_custom_fusion = f32[65]{0:T(128)S(1)} fusion(s32[2048]{0:T(1024)S(1)} %and_select_fusion, f32[2048]{0:T(1024)S(1)} %broadcast.95, f32[]{:T(128)} %constant.76.clone.1), kind=kCustom, calls=%fused_computation.59 | custom fusion | flops 2048 | bytes 264 | tf_op jit(solution)/shard_map/scatter-add | solution.py:31
  53.5 126.3 %reduce-scatter.4.cloned.1.call-done = f32[64,128]{1,0:T(8,128)} async-done(((f32[4096,128]{1,0:T(8,128)}), f32[64,128]{1,0:T(8,128)}) %reduce-scatter.4.cloned.1.call-update) | async-done | bytes 32784
  179.7 0.8 copy.15
  180.6 0.9 fusion.46
  181.6 240.4 %all-reduce.5.cloned.1.call-done = f32[128,128]{0,1:T(8,128)} async-done(((f32[128,128]{0,1:T(8,128)}), f32[128,128]{0,1:T(8,128)}) %all-reduce.5.cloned.1.call-update) | async-done | bytes 65552 | tf_op jit(solution)/shard_map/psum | solution.py:63
  422.0 0.9 copy.11
  423.0 0.9 fusion.22
  423.8 11.7 %custom-call.14 = f32[128,128]{1,0:T(8,128)S(1)} custom-call(f32[128,128]{1,0:T(8,128)S(1)} %fusion.22), custom_call_target="Cholesky" | custom-call | tf_op jit(solution)/shard_map/jvp(jit(cholesky))/cholesky/custom-call.1 | solution.py:35
  435.6 0.7 compare_reduce_fusion
  436.2 0.6 fusion.24
  436.9 9.8 %custom-call.13 = f32[1,128,128]{1,2,0:T(8,128)S(1)} custom-call(f32[1,128,128]{2,1,0:T(8,128)S(1)} %fusion.24), custom_call_target="InvertDiagBlocksLowerTriangular" | custom-call | tf_op jit(solution)/shard_map/transpose(jvp(jit(cholesky)))/triangular_solve | solution.py:35
  446.7 0.2 fusion.20
  446.9 0.3 fusion.47
  447.2 1.0 fusion.29
  448.2 0.2 all-gather.2.cloned.1.call-start
  448.5 0.3 fusion.48
  448.7 233.9 %all-reduce.7.cloned.1.call-done = f32[128,128]{1,0:T(8,128)} async-done(((f32[128,128]{1,0:T(8,128)}), f32[128,128]{1,0:T(8,128)}) %all-reduce.7.cloned.1.call-update) | async-done | bytes 65552 | tf_op jit(solution)/shard_map/psum | solution.py:66
  682.6 1.1 fusion.1
  683.7 0.9 fusion
  684.6 0.2 fusion.18
  684.9 0.3 fusion.16
  685.2 0.3 fusion.12
  685.5 0.9 fusion.3
  686.4 72.9 %all-gather.2.cloned.1.call-done = bf16[4096,128]{1,0:T(8,128)(2,1)} async-done(((bf16[64,128]{1,0:T(8,128)(2,1)}), bf16[4096,128]{1,0:T(8,128)(2,1)}) %all-gather.2.cloned.1.call-update) | async-done | bytes 1048592 | tf_op jit(solution)/shard_map/all_gather | solution.py:76
  759.3 5.2 convolution_bitcast_fusion.1
  764.5 21.6 %all-reduce.9 = bf16[576,128]{0,1:T(8,128)(2,1)S(1)} all-reduce(f32[576,128]{0,1:T(8,128)} %convolution_bitcast_fusion.1), channel_id=1, replica_groups=mesh['example'=64,'feature'=4] {'feature'}, use_global_device_ids=true, to_apply=%region_7.9 | all-reduce | flops 73728 | bytes 442368 | tf_op jit(solution)/shard_map/psum | solution.py:77
  786.1 1.4 fusion.49
  787.5 3.6 add_convert_fusion
  (24 shorter events, 0.4 us)
Async XLA Ops:
  6.5 32.1 %copy-start = (s32[4096,128]{1,0:T(8,128)S(1)}, s32[4096,128]{1,0:T(8,128)}, u32[]{:S(2)}) copy-start(s32[4096,128]{1,0:T(8,128)} %param.7) | copy-start | bytes 6291460
  6.5 173.2 %reduce-scatter.4.cloned.1.call-start = ((), (), s32[]{:S(2)}) async-start(), calls=%async_computation.4 | async-start | bytes 2129920
  35.6 3.2 copy-start.3
  38.6 383.5 %all-reduce.5.cloned.1.call-start = ((), (), s32[]{:S(2)}) async-start(), calls=%async_computation.1 | async-start | bytes 131072 | tf_op jit(solution)/shard_map/psum | solution.py:63
  181.5 501.1 %all-reduce.7.cloned.1.call-start = ((), (), s32[]{:S(2)}) async-start(), calls=%async_computation.2 | async-start | bytes 131072 | tf_op jit(solution)/shard_map/psum | solution.py:66
  448.2 311.1 %all-gather.2.cloned.1.call-start = ((), (), s32[]{:S(2)}) async-start(), calls=%async_computation.3 | async-start | bytes 1064960 | tf_op jit(solution)/shard_map/all_gather | solution.py:76
  759.3 26.8 %copy-start.1 = (bf16[4096,128]{1,0:T(8,128)(2,1)S(1)}, bf16[4096,128]{1,0:T(8,128)(2,1)}, u32[]{:S(2)}) copy-start(bf16[4096,128]{1,0:T(8,128)(2,1)} %all-gather.2.cloned.1.call-done) | copy-start | bytes 3145732
  786.1 1.4 copy-start.2
Sparse Core Ops, SparseCore 0:
  38.7 140.9 reduce-scatter.3
  186.1 235.8 all-reduce.4
  448.3 234.2 all-reduce.6
  686.6 72.6 all-gather.1
where the time goes:
time: 798 us
  waiting for transfers between devices  674 us (84%)
  blocking collectives  41.8 us (5%)
  other arithmetic  38.4 us (5%)
  matrix products  25.4 us (3%)
  between operations  13.3 us (2%)
    psum x1, waiting for transfers between devices, on_device(): lax.psum(transposed(image, image, HIGH), ('example', 'feature'))  240 us
    psum x1, waiting for transfers between devices, on_device(): lax.psum(transposed(orthonormal * row_counts[:, None], orthonormal, HIGH)...  234 us
    unnamed x5, waiting for transfers between devices  126 us
    all_gather x1, waiting for transfers between devices, on_device(): grad_low = lax.all_gather(grad_low, 'example', axis=0, tiled=True)  72.9 us
    another operation x5, other arithmetic, upper_factor(): return jnp.linalg.cholesky(gram_matrix).T  22.8 us
    psum x1, blocking collectives, on_device(): lax.psum(jnp.dot(embeddings, grad_low, preferred_element_type=jnp.float32...  21.6 us
    psum x1, blocking collectives, on_device(): lax.psum(jnp.dot(embeddings, subspace, preferred_element_type=jnp.float32...  20.2 us
  transfers between devices with their start and end apart: 4, of which 4 were waited for; matrix products, arithmetic and copies ran while one was open for 2% of the time, Pallas kernels for 0%

commit v1 on v0

--- a/solution.py
+++ b/solution.py
@@ -5,6 +5,12 @@
 
 NOISE_STEP = 1.0 / 4096.0
 HIGH = lax.Precision.HIGHEST
+
+
+def gather_from_all(x, axis, dim):
+    length = lax.axis_size(axis)
+    repeats = [length if d == dim else 1 for d in range(x.ndim)]
+    return lax.all_to_all(jnp.tile(x, repeats), axis, split_axis=dim, concat_axis=dim, tiled=True)
 
 
 def transposed(former, latter, precision=None):
@@ -73,7 +79,7 @@
         :, None
     ] * jnp.dot(image, gram_inverse, precision=HIGH)
     grad_low = image_grad.astype(jnp.bfloat16)
-    grad_low = lax.all_gather(grad_low, "example", axis=0, tiled=True)
+    grad_low = gather_from_all(grad_low, "example", 0)
     back_sum = lax.psum(
         jnp.dot(embeddings, grad_low, preferred_element_type=jnp.float32), "feature"
     )

time: 798 us -> 765 us (0.959)
  waiting for transfers between devices: 674 us -> 601 us
  blocking collectives: 41.8 us -> 75 us
    all_gather x1 -> x0, waiting for transfers between devices: 72.9 us -> none  [on_device(): grad_low = lax.all_gather(grad_low, 'example', axis=0, tiled=True)]
    all_to_all x0 -> x1, blocking collectives: none -> 33.8 us  [gather_from_all(): lax.all_to_all(jnp.tile(x, repeats), axis, split_axis=dim, concat_axis=di...]
    unnamed x5 -> x4, waiting for transfers between devices: 126 us -> 126 us
  transfers between devices with their start and end apart: 4 -> 3, of which waited for: 4 -> 3; matrix products, arithmetic and copies ran while one was open for 2% -> 2% of each run, Pallas kernels for 0% -> 0%
where the time goes in v1:
time: 765 us; the launch traced here: 764 us
  waiting for transfers between devices  601 us (79%)
  blocking collectives  75 us (10%)
  other arithmetic  38.4 us (5%)
  matrix products  31.4 us (4%)
  between operations  13.3 us (2%)
    psum x1, waiting for transfers between devices, on_device(): lax.psum(transposed(image, image, HIGH), ('example', 'feature'))  240 us
    psum x1, waiting for transfers between devices, on_device(): lax.psum(transposed(orthonormal * row_counts[:, None], orthonormal, HIGH)...  234 us
    unnamed x4, waiting for transfers between devices  126 us
    all_to_all x1, blocking collectives, gather_from_all(): lax.all_to_all(jnp.tile(x, repeats), axis, split_axis=dim, concat_axis=di...  33.8 us
    another operation x5, other arithmetic, upper_factor(): return jnp.linalg.cholesky(gram_matrix).T  22.8 us
    psum x1, blocking collectives, on_device(): lax.psum(jnp.dot(embeddings, grad_low, preferred_element_type=jnp.float32...  21.1 us
    psum x1, blocking collectives, on_device(): lax.psum(jnp.dot(embeddings, subspace, preferred_element_type=jnp.float32...  20.2 us
  transfers between devices with their start and end apart: 3, of which 3 were waited for; matrix products, arithmetic and copies ran while one was open for 2% of the time, Pallas kernels for 0%

profile of v1, /device:TPU:2, one launch (start us, length us, event | category | flops | bytes accessed | tf_op | source)
XLA Modules:
  0.0 764.2 jit_solution(2596139925950020157)
XLA Ops:
  6.5 4.2 fusion.45
  10.7 20.2 %all-reduce.8 = bf16[576,128]{1,0:T(8,128)(2,1)S(1)} all-reduce(f32[576,128]{1,0:T(8,128)S(1)} %fusion.45), channel_id=1, replica_groups=mesh['example'=64,'feature'=4] {'feature'}, use_global_device_ids=true, to_apply=%region_0.0 | all-reduce | flops 73728 | bytes 442368 | tf_op jit(solution)/shard_map/psum | solution.py:56
  30.9 4.7 convolution_bitcast_fusion
  35.6 2.9 copy.14
  38.8 14.7 %scatter_custom_fusion = f32[65]{0:T(128)S(1)} fusion(s32[2048]{0:T(1024)S(1)} %and_select_fusion, f32[2048]{0:T(1024)S(1)} %broadcast.98, f32[]{:T(128)} %constant.76.clone.1), kind=kCustom, calls=%fused_computation.59 | custom fusion | flops 2048 | bytes 264 | tf_op jit(solution)/shard_map/scatter-add | solution.py:37
  53.5 126.3 %reduce-scatter.4.cloned.1.call-done = f32[64,128]{1,0:T(8,128)} async-done(((f32[4096,128]{1,0:T(8,128)}), f32[64,128]{1,0:T(8,128)}) %reduce-scatter.4.cloned.1.call-update) | async-done | bytes 32784
  179.7 0.8 copy.15
  180.6 0.9 fusion.46
  181.5 0.2 all-reduce.7.cloned.1.call-start
  181.8 240.3 %all-reduce.5.cloned.1.call-done = f32[128,128]{0,1:T(8,128)} async-done(((f32[128,128]{0,1:T(8,128)}), f32[128,128]{0,1:T(8,128)}) %all-reduce.5.cloned.1.call-update) | async-done | bytes 65552 | tf_op jit(solution)/shard_map/psum | solution.py:69
  422.0 0.9 copy.11
  423.0 0.9 fusion.22
  423.8 11.7 %custom-call.14 = f32[128,128]{1,0:T(8,128)S(1)} custom-call(f32[128,128]{1,0:T(8,128)S(1)} %fusion.22), custom_call_target="Cholesky" | custom-call | tf_op jit(solution)/shard_map/jvp(jit(cholesky))/cholesky/custom-call.1 | solution.py:41
  435.6 0.7 compare_reduce_fusion
  436.2 0.6 fusion.24
  436.9 9.8 %custom-call.13 = f32[1,128,128]{1,2,0:T(8,128)S(1)} custom-call(f32[1,128,128]{2,1,0:T(8,128)S(1)} %fusion.24), custom_call_target="InvertDiagBlocksLowerTriangular" | custom-call | tf_op jit(solution)/shard_map/transpose(jvp(jit(cholesky)))/triangular_solve | solution.py:41
  446.7 0.2 fusion.20
  446.9 0.3 fusion.47
  447.2 1.0 fusion.29
  448.2 0.3 fusion.48
  448.5 234.1 %all-reduce.7.cloned.1.call-done = f32[128,128]{1,0:T(8,128)} async-done(((f32[128,128]{1,0:T(8,128)}), f32[128,128]{1,0:T(8,128)}) %all-reduce.7.cloned.1.call-update) | async-done | bytes 65552 | tf_op jit(solution)/shard_map/psum | solution.py:72
  682.6 1.1 fusion.1
  683.7 0.9 fusion
  684.9 0.3 fusion.16
  685.2 0.3 fusion.12
  685.5 0.3 fusion.3
  685.8 0.2 tile.2
  686.1 33.8 %all_to_all.9 = bf16[64,64,128]{2,1,0:T(8,128)(2,1)S(1)} all-to-all(bf16[64,64,128]{2,1,0:T(8,128)(2,1)S(1)} %tile.2), channel_id=1, replica_groups=mesh['example'=64,'feature'=4] {'example'}, dimensions={0} | all-to-all | bytes 2097152 | tf_op jit(solution)/shard_map/all_to_all | solution.py:13
  719.8 4.1 convolution_bitcast_fusion.1
  724.0 5.0 fusion.49
  729.0 21.1 %all-reduce.9 = bf16[576,128]{0,1:T(8,128)(2,1)S(1)} all-reduce(f32[576,128]{0,1:T(8,128)S(1)} %convolution_bitcast_fusion.1), channel_id=1, replica_groups=mesh['example'=64,'feature'=4] {'feature'}, use_global_device_ids=true, to_apply=%region_7.9 | all-reduce | flops 73728 | bytes 442368 | tf_op jit(solution)/shard_map/psum | solution.py:83
  750.1 7.6 add_convert_fusion
  (19 shorter events, 0.6 us)
Async XLA Ops:
  6.5 32.1 %copy-start = (s32[4096,128]{1,0:T(8,128)S(1)}, s32[4096,128]{1,0:T(8,128)}, u32[]{:S(2)}) copy-start(s32[4096,128]{1,0:T(8,128)} %param.7) | copy-start | bytes 6291460
  6.5 173.2 %reduce-scatter.4.cloned.1.call-start = ((), (), s32[]{:S(2)}) async-start(), calls=%async_computation.4 | async-start | bytes 2129920
  35.6 3.2 copy-start.1
  38.6 383.5 %all-reduce.5.cloned.1.call-start = ((), (), s32[]{:S(2)}) async-start(), calls=%async_computation.2 | async-start | bytes 131072 | tf_op jit(solution)/shard_map/psum | solution.py:69
  181.5 501.1 %all-reduce.7.cloned.1.call-start = ((), (), s32[]{:S(2)}) async-start(), calls=%async_computation.3 | async-start | bytes 131072 | tf_op jit(solution)/shard_map/psum | solution.py:72
Sparse Core Ops, SparseCore 0:
  38.7 140.9 reduce-scatter.3
  186.1 235.8 all-reduce.4
  448.3 234.2 all-reduce.6
